TPU v7x, 512 devices: a whole 4x4x16 slice. The times are simulated.
512 devices in a mesh: dp: 4 (over y), row: 16 (over z), col: 8 (over x, core).
Axes of the slice: x: 4, y: 4, z: 16, core: 2. Of those that a mesh axis runs over, the one named last changes fastest.
Arguments:
- activations: bfloat16 [4, 3072, 4096], P('dp', 'col', 'row'), may hold values from -6 to 6
- out_grads: bfloat16 [4, 3072, 14336], P('dp', 'row', 'col'), may hold values from -0.078125 to 0.078125
- query_ids: int32 [4, 3072], P('dp'), may hold values from 0 to 383, never falling along the last dimension, each value on 1 to 32 neighbouring positions
- clip_bound: int32 [1], replicated, may hold values from 160 to 459
Outputs:
- weight_grad: float32 [4096, 14336], P('row', 'col')
Inputs may be any that keep to these rules, and one draw needn't show every extreme that they name: `query_ids`: within each data group the ids never fall along the tokens; each query holds 1 to 32 consecutive tokens, and one holds exactly 32.
All inputs are finite; a program needn't handle non-finite values.
Results may differ from a plain program's by a relative error of at most 0.0003.
The roundings to bfloat16 on the way count: a program that leaves them out, or rounds other values in their place, can miss the bound.
Values may be sent and summed in bfloat16 or wider, within the bound.
A program may use at most 64 MiB of HBM per device.

v0:
```python
import functools

import jax
import jax.numpy as jnp
from jax import lax
from jax.experimental import pallas as pl
from jax.experimental.pallas import tpu as pltpu
from jax.sharding import PartitionSpec as P

TILE = 32
LANES = 128
WIDTHS = (256, 256, 256, 128, 256, 256, 256, 128)
FIRST_SLOTS = (0, 0, 0, 1, 4, 5, 7, 8)
STAGE_GAP = 3
MESH = pl.DeviceIdType.MESH


def packed(products):
    lane = lax.broadcasted_iota(jnp.int32, (TILE, LANES), 1)
    row = lax.broadcasted_iota(jnp.int32, (TILE, LANES), 0)
    near = jnp.where(lane <= row, pltpu.roll(products, LANES - TILE, 1), products)
    group = lax.broadcasted_iota(jnp.int32, (8, LANES), 1) // TILE
    out = near[:8]
    for k in range(1, 4):
        out = jnp.where(group == k, pltpu.roll(near[8 * k : 8 * k + 8], TILE * k, 1), out)
    return out


def kernel(
    sizes,
    x_ref, g_ref, ids_ref, clip_ref,
    out_ref,
    ids_vmem, bands, gbuf, xbuf, st, idcol, rows,
    asend, abuf, bsend, bbuf, wz, wall,
    pbuf, rfar, rnear, qbuf, rdir,
    lsem, osem, xs, xr, hs, rs, rr, asem, arec, bsem, brec, wsem, wrec, zsem, zrec,
    s1, r1, s2, r2, s3, r3, s4, r4, sd,
):
    ny, nz, nw, tokens = sizes
    nx = nw // 2
    tz = g_ref.shape[0]
    tc = x_ref.shape[0]
    tiles = tz // TILE
    chunks = len(WIDTHS)
    columns = [pl.ds(sum(WIDTHS[:c]), WIDTHS[c]) for c in range(chunks)]
    steps = nz // 2
    wide = bands.shape[1]
    blocks = tokens // LANES
    part = x_ref.shape[1] // ny

    y = lax.axis_index("dp")
    z = lax.axis_index("row")
    w = lax.axis_index("col")
    core = lax.rem(w, 2)
    chip = w // 2

    def z_at(d):
        return lax.rem(z + d, nz)

    def w_at(d):
        return lax.rem(w + d, nw)

    def y_at(d):
        return lax.rem(y + d, ny)

    def copy_to(src, dst, send, recv, **axis):
        return pltpu.make_async_remote_copy(
            src_ref=src, dst_ref=dst, send_sem=send, recv_sem=recv,
            device_id=axis, device_id_type=MESH,
        )

    own_rows = pl.ds(pl.multiple_of(z * tz, 32), tz)
    own_g = [
        pltpu.make_async_copy(
            g_ref.at[:, columns[c]], gbuf[c].at[own_rows], lsem.at[c]
        )
        for c in range(chunks)
    ]
    own_x = pltpu.make_async_copy(
        x_ref, xbuf.at[pl.ds(pl.multiple_of(TILE + w * tc, 32), tc)], lsem.at[chunks]
    )
    own_ids = pltpu.make_async_copy(ids_ref, ids_vmem, lsem.at[chunks + 1])
    for copy in own_g:
        copy.start()
    own_x.start()
    own_ids.start()

    barrier = pltpu.get_barrier_semaphore()
    for d in range(1, nz):
        pl.semaphore_signal(barrier, inc=1, device_id={"row": z_at(d)}, device_id_type=MESH)
    for d in range(1, nw):
        pl.semaphore_signal(barrier, inc=1, device_id={"col": w_at(d)}, device_id_type=MESH)
    for d in range(1, ny):
        pl.semaphore_signal(barrier, inc=1, device_id={"dp": y_at(d)}, device_id_type=MESH)
    pl.semaphore_wait(barrier, nz + nw + ny - 3)

    def x_rows(owner):
        return xbuf.at[pl.ds(pl.multiple_of(TILE + owner * tc, 32), tc)]

    sibling = chip * 2 + 1 - core

    def x_first(d):
        to = sibling if d == 0 else lax.rem(chip + d, nx) * 2 + core
        return copy_to(x_ref, x_rows(w), xs.at[d], xr.at[d], col=to)

    def x_came(d):
        owner = sibling if d == 0 else lax.rem(chip + nx - d, nx) * 2 + core
        return copy_to(x_rows(owner), x_rows(owner), xs.at[d], xr.at[d], col=sibling)

    def x_forward(d):
        owner = lax.rem(chip + nx - d, nx) * 2 + core
        return copy_to(
            x_rows(owner), x_rows(owner), xs.at[nx - 1 + d], xr.at[nx - 1 + d], col=sibling
        )

    def x_forwarded(d):
        owner = lax.rem(chip + nx - d, nx) * 2 + 1 - core
        return copy_to(
            x_rows(owner), x_rows(owner), xs.at[nx - 1 + d], xr.at[nx - 1 + d], col=sibling
        )

    def ring(way, c, s, incoming=False):
        hop = s + 1 if incoming else s
        owner = z_at(nz - hop) if way == 0 else z_at(hop)
        skip, count = 0, tz
        if s == steps - 1:
            skip, count = way * (tz // 2), tz // 2
        elif s == 0 and way == 0:
            count = tz - TILE
        block = gbuf[c].at[pl.ds(pl.multiple_of(owner * tz + skip, 32), count)]
        src = block
        if s == 0 and not incoming:
            src = g_ref.at[pl.ds(0, count), columns[c]]
        to = z_at(1) if way == 0 else z_at(nz - 1)
        return copy_to(src, block, rs.at[way, c, s], rr.at[way, c, s], row=to)

    def halo_copy(c, incoming=False):
        owner = z_at(nz - 1) if incoming else z
        there = gbuf[c].at[pl.ds(pl.multiple_of(owner * tz + tz - TILE, 32), TILE)]
        src = there if incoming else g_ref.at[pl.ds(tz - TILE, TILE), columns[c]]
        return copy_to(src, there, hs.at[0, c], hs.at[1, c], row=z_at(1))

    def act_send(d):
        return copy_to(asend.at[d], abuf.at[d], asem.at[d], arec.at[d], row=z_at(d))

    def grad_send(j):
        return copy_to(bsend.at[j], bbuf.at[w], bsem.at[j], brec.at[w], col=j)

    def grad_came(owner):
        return copy_to(bbuf.at[owner], bbuf.at[owner], bsem.at[0], brec.at[owner], col=w_at(1))

    def weight_send(d):
        return copy_to(wz.at[z], wz.at[z], zsem.at[d], zrec.at[d], row=z_at(d))

    def weight_came(d):
        owner = z_at(nz - d)
        return copy_to(wz.at[owner], wz.at[owner], zsem.at[d], zrec.at[d], row=z_at(1))

    def slab_send(d):
        return copy_to(wz, wall.at[w], wsem.at[d], wrec.at[w], col=w_at(d))

    def slab_came(owner):
        return copy_to(wall.at[owner], wall.at[owner], wsem.at[1], wrec.at[owner], col=w_at(1))

    up, far, down = y_at(1), y_at(2), y_at(3)
    half = part // 2

    def quarter(owner, side=None):
        if side is None:
            return pl.ds(pl.multiple_of(owner * part, part), part)
        return pl.ds(pl.multiple_of(owner * part + side * half, half), half)

    def far_send(c, side):
        return copy_to(
            pbuf[c].at[quarter(far, side)], rfar[c].at[side], s1.at[c, side], r1.at[c, side],
            dp=(up, down)[side],
        )

    def near_send(c, side):
        to = (up, down)[side]
        return copy_to(
            pbuf[c].at[quarter(to)], rnear[c].at[side], s2.at[c, side], r2.at[c, side], dp=to
        )

    def out_at(c, where):
        return out_ref.at[where, columns[c]]

    def out_send(c, side, incoming=False):
        at = out_at(c, quarter((down, up)[side] if incoming else y))
        return copy_to(
            at if incoming else qbuf[c], at, s3.at[c, side], r3.at[c, side],
            dp=(up, down)[side],
        )

    def out_forward(c, side, incoming=False):
        at = out_at(c, quarter(far if incoming else (down, up)[side], side))
        return copy_to(at, at, s4.at[c, side], r4.at[c, side], dp=(up, down)[side])

    def direct_send(c, d):
        to = y_at(d)
        return copy_to(
            pbuf[c].at[quarter(to)], rdir.at[d - 1], sd.at[0, d - 1], sd.at[1, d - 1], dp=to
        )

    def direct_out(c, d, incoming=False):
        at = out_at(c, quarter(y_at(ny - d) if incoming else y))
        return copy_to(
            at if incoming else qbuf[c], at, sd.at[2, d - 1], sd.at[3, d - 1], dp=y_at(d)
        )

    def out_own(c):
        return pltpu.make_async_copy(qbuf[c], out_at(c, quarter(y)), osem.at[c])

    def product(c):
        depth = tokens // 3 if tokens % (3 * LANES) == 0 else LANES
        for k in range(tokens // depth):
            at = pl.ds(k * depth, depth)
            term = jnp.dot(st[:, at], gbuf[c][at], preferred_element_type=jnp.float32)
            pbuf[c][...] = term if k == 0 else pbuf[c][...] + term
        for side in range(2):
            far_send(c, side).start()

    def product_pair(c, i):
        pair = lax.rem(lax.rem(z + steps, nz) // 2 + i, steps)
        at = pl.ds(pl.multiple_of(pair * 2 * tz, LANES), 2 * tz)
        return jnp.dot(st[:, at], gbuf[c][at], preferred_element_type=jnp.float32)

    def product_most(c):
        pbuf[c][...] = product_pair(c, 1)

        def one(i, carry):
            pbuf[c][...] = pbuf[c][...] + product_pair(c, i)
            return carry

        lax.fori_loop(2, steps, one, 0)

    def product_rest(c):
        pbuf[c][...] = pbuf[c][...] + product_pair(c, 0)
        for d in range(1, ny):
            direct_send(c, d).start()

    def direct_finish(c):
        total = pbuf[c][quarter(y)]
        for d in range(1, ny):
            direct_send(c, d).wait_recv()
            total = total + rdir[d - 1]
        qbuf[c][...] = total
        for d in range(1, ny):
            direct_out(c, d).start()
        out_own(c).start()

    def direct_done(c):
        for d in range(1, ny):
            direct_out(c, d, incoming=True).wait_recv()
            direct_send(c, d).wait_send()
            direct_out(c, d).wait_send()
        out_own(c).wait()

    def near(c):
        for side in range(2):
            far_send(c, side).wait_recv()
            where = quarter((up, down)[side], side)
            pbuf[c][where] = pbuf[c][where] + rfar[c][side]
            near_send(c, side).start()

    def finish(c):
        total = pbuf[c][quarter(y)]
        for side in range(2):
            near_send(c, side).wait_recv()
            total = total + rnear[c][side]
        qbuf[c][...] = total
        for side in range(2):
            out_send(c, side).start()
        out_own(c).start()

    def forward_out(c):
        for side in range(2):
            out_send(c, side, incoming=True).wait_recv()
            out_forward(c, side).start()

    def out_done(c):
        for side in range(2):
            out_forward(c, side, incoming=True).wait_recv()
            far_send(c, side).wait_send()
            near_send(c, side).wait_send()
            out_send(c, side).wait_send()
            out_forward(c, side).wait_send()
        out_own(c).wait()

    def prepare():
        own_ids.wait()
        idcol[0:TILE] = jnp.full((TILE, LANES), -1.0, jnp.float32)
        xbuf[0:TILE] = jnp.zeros((TILE, xbuf.shape[1]), xbuf.dtype)
        lane = lax.broadcasted_iota(jnp.int32, (8, LANES), 1)
        none = jnp.full((8, LANES), -1.0, jnp.float32)
        flat = []
        for b in range(blocks):
            row = ids_vmem[0:1, b * LANES : (b + 1) * LANES].astype(jnp.float32)
            flat.append(jnp.broadcast_to(row, (8, LANES)))
            idcol[TILE + b * LANES : TILE + (b + 1) * LANES] = jnp.broadcast_to(
                row, (LANES, LANES)
            ).T
        for b in range(blocks):
            before = flat[b - 1] if b > 0 else none
            after = flat[b + 1] if b < blocks - 1 else none
            rows[0, b] = flat[b]
            rows[1, b] = jnp.where(
                lane < TILE, after, jnp.where(lane >= LANES - TILE, before, none)
            )

    def grad_bands():
        before = pl.ds(pl.multiple_of(z_at(nz - 1) * tz + tz - TILE, 32), TILE)
        dims = (((1,), (1,)), ((), ()))
        band = jnp.zeros((tz, wide), jnp.float32)
        for c in range(chunks):
            own = gbuf[c][own_rows]
            pad = jnp.zeros((wide - tz - TILE, WIDTHS[c]), own.dtype)
            window = jnp.concatenate([gbuf[c][before], own, pad], 0)
            band = band + lax.dot_general(own, window, dims, preferred_element_type=jnp.float32)
        bands[...] = band
        for j in range(tiles):
            turned = bands[j * TILE : (j + 1) * TILE]
            if j > 0:
                turned = pltpu.roll(turned, wide - j * TILE, 1)
            bsend[j] = packed(turned[:, :LANES])
            @pl.when(w != j)
            def _():
                grad_send(j).start()

    def act_bands():
        x_came(0).wait_recv()
        for d in range(1, nx):
            x_forwarded(d).wait_recv()

        @pl.when(w < tiles)
        def _():
            def one(d, carry):
                first = pl.multiple_of(z_at(d) * tz + w * TILE, 32)
                window = xbuf[pl.ds(first, 2 * TILE)]
                window = jnp.concatenate([window, jnp.zeros_like(window)], 0)
                dims = (((1,), (1,)), ((), ()))
                asend[d] = packed(
                    lax.dot_general(
                        window[TILE : 2 * TILE], window, dims, preferred_element_type=jnp.float32
                    )
                )
                @pl.when(d > 0)
                def _():
                    act_send(d).start()
                return carry
            lax.fori_loop(0, nz, one, 0)

    def weights():
        @pl.when(w < tiles)
        def _():
            act = asend[0]
            for d in range(1, nz):
                act_send(d).wait_recv()
                act = act + abuf[d]
            bbuf[w] = bsend[w]
            for d in range(1, nw):
                grad_came(w_at(d)).wait_recv()
            grad = bbuf[0]
            for u in range(1, nw):
                grad = grad + bbuf[u]
            tile = z * tiles + w
            first = pl.multiple_of(tile * TILE, 32)
            ids = idcol[pl.ds(first, 2 * TILE)]
            lane = lax.broadcasted_iota(jnp.int32, (8, LANES), 1)
            row = lax.broadcasted_iota(jnp.int32, (8, LANES), 0)
            group, partner = lane // TILE, lax.rem(lane, TILE)
            token = row + 8 * group
            mine = ids[TILE : TILE + 8]
            for k in range(1, 4):
                mine = jnp.where(group == k, ids[TILE + 8 * k : TILE + 8 * k + 8], mine)
            wide_lane = lax.broadcasted_iota(jnp.int32, (TILE, LANES), 1)
            wide_row = lax.broadcasted_iota(jnp.int32, (TILE, LANES), 0)
            pick = lax.rem(wide_lane, TILE) == wide_row
            before = jnp.sum(jnp.where(pick, ids[:TILE], 0.0), 0, keepdims=True)
            same = jnp.sum(jnp.where(pick, ids[TILE:], 0.0), 0, keepdims=True)
            theirs = jnp.where(partner <= token, same, before)
            factor = jnp.where(partner == token, 1.0, 2.0)
            factor = jnp.where(partner <= token, factor, jnp.where(tile > 0, 2.0, 0.0))
            term = jnp.where(mine == theirs, act * grad * factor, 0.0)
            at = lax.rem(tile, LANES // TILE) * TILE
            spread = jnp.zeros((8, LANES), jnp.float32)
            for k in range(4):
                one = jnp.sum(jnp.where(group == k, term, 0.0), 1, keepdims=True)
                spread = spread + jnp.where(lane == row + 8 * k + at, one, 0.0)
            wz[z] = jnp.sum(spread, 0, keepdims=True)
            for d in range(1, nz):
                weight_send(d).start()

    def slabs():
        @pl.when(w < tiles)
        def _():
            for d in range(1, nz):
                weight_came(d).wait_recv()
            wall[w] = wz[...]
            for d in range(1, nw):
                slab_send(d).start()

    def scales():
        for u in range(tiles):
            @pl.when(w != u)
            def _():
                slab_came(u).wait_recv()
        lane = lax.broadcasted_iota(jnp.int32, (8, LANES), 1)
        none = jnp.zeros((8, LANES), jnp.float32)
        flat = []
        for b in range(blocks):
            row = none
            for k in range(b * (LANES // TILE), (b + 1) * (LANES // TILE)):
                owner, j = divmod(k, tiles)
                row = row + jnp.broadcast_to(wall[j, owner], (8, LANES))
            flat.append(row)
        for b in range(blocks):
            before = flat[b - 1] if b > 0 else none
            after = flat[b + 1] if b < blocks - 1 else none
            rows[2, b] = flat[b]
            rows[3, b] = jnp.where(
                lane < TILE, after, jnp.where(lane >= LANES - TILE, before, none)
            )
        limit = clip_ref[0].astype(jnp.float32)

        def one(b, carry):
            at = pl.multiple_of(TILE + b * LANES, 32)
            ids = idcol[pl.ds(at, LANES)]
            found = jnp.where(ids == rows[0, b][0:1], rows[2, b][0:1], 0.0)
            found = found + jnp.where(ids == rows[1, b][0:1], rows[3, b][0:1], 0.0)
            squares = jnp.sum(found, 1, keepdims=True)
            factor = limit / jnp.maximum(jnp.sqrt(jnp.maximum(squares, 0.0)), limit)
            scaled = xbuf[pl.ds(at, LANES)].astype(jnp.float32) * factor
            st[:, pl.ds(pl.multiple_of(b * LANES, LANES), LANES)] = scaled.T.astype(st.dtype)
            return carry

        lax.fori_loop(0, blocks, one, 0)

    def forward_x():
        for d in range(1, nx):
            x_came(d).wait_recv()
            x_forward(d).start()

    first_slot = FIRST_SLOTS
    final_slot = first_slot[-1] + steps
    between = {0: (prepare,), 1: (grad_bands,), 2: (forward_x,), 3: (act_bands,), 5: (weights,),
               6: (slabs,), 7: (scales,)}

    def ring_sent(c):
        for s in range(steps):
            for way in range(2):
                ring(way, c, s).wait_send()

    def hop(t, c):
        s = t - first_slot[c]
        if 0 <= s < steps:
            for way in range(2):
                if s > 0:
                    ring(way, c, s - 1, incoming=True).wait_recv()
                ring(way, c, s).start()

    def first(c):
        for way in range(2):
            ring(way, c, steps - 1, incoming=True).wait_recv()
        if c == chunks - 1:
            product_rest(c)
        else:
            product(c)
        ring_sent(c)

    def stages(p):
        for c in range(chunks):
            calls = (first, near, finish, forward_out, out_done)
            if c == chunks - 1:
                calls = (first, direct_finish, direct_done)
            stage, rest = divmod(p - 2 * (first_slot[c] + steps) - c % 2, STAGE_GAP)
            if 0 <= stage < len(calls) and rest == 0:
                calls[stage](c)

    for t in range(final_slot):
        if t == 1:
            for c in range(chunks):
                halo_copy(c, incoming=True).wait_recv()
                own_g[c].wait()
        for c in range(0, chunks, 2):
            hop(t, c)
        if t == 0:
            for d in range(nx):
                x_first(d).start()
            for c in range(chunks):
                halo_copy(c).start()
            own_x.wait()
        for step in between.get(t, ()):
            step()
        stages(2 * t)
        for c in range(1, chunks, 2):
            hop(t, c)
        stages(2 * t + 1)
    product_most(chunks - 1)

    for c in range(chunks):
        halo_copy(c).wait_send()
    for d in range(nx):
        x_first(d).wait_send()
    for d in range(1, nx):
        x_forward(d).wait_send()
    for j in range(tiles):
        @pl.when(w != j)
        def _():
            grad_send(j).wait_send()

    @pl.when(w < tiles)
    def _():
        for d in range(1, nz):
            act_send(d).wait_send()
            weight_send(d).wait_send()
        for d in range(1, nw):
            slab_send(d).wait_send()

    for p in range(2 * final_slot, 2 * final_slot + 5 * STAGE_GAP):
        stages(p)


def body(sizes, activations, out_grads, query_ids, clip_bound):
    x_local = activations[0]
    g_local = out_grads[0]
    ny, nz, nw, tokens = sizes
    nx = nw // 2
    features, hidden = x_local.shape[1], g_local.shape[1]
    tz = g_local.shape[0]
    tiles = tz // TILE
    chunks = len(WIDTHS)
    assert sum(WIDTHS) == hidden
    steps = nz // 2
    part = features // ny
    dma = pltpu.SemaphoreType.DMA
    f32, bf16 = jnp.float32, jnp.bfloat16
    stay = [
        pltpu.with_memory_space_constraint(a, pltpu.HBM) for a in (x_local, g_local, query_ids)
    ]
    return pl.pallas_call(
        functools.partial(kernel, sizes),
        out_shape=jax.ShapeDtypeStruct((features, hidden), f32),
        in_specs=[
            pl.BlockSpec(memory_space=pltpu.HBM),
            pl.BlockSpec(memory_space=pltpu.HBM),
            pl.BlockSpec(memory_space=pltpu.HBM),
            pl.BlockSpec(memory_space=pltpu.SMEM),
        ],
        out_specs=pl.BlockSpec(memory_space=pl.ANY),
        scratch_shapes=[
            pltpu.VMEM((1, tokens), jnp.int32),
            pltpu.VMEM((tz, -(-(tz + TILE) // LANES) * LANES), f32),
            [pltpu.VMEM((tokens, n), bf16) for n in WIDTHS],
            pltpu.VMEM((TILE + tokens, features), bf16),
            pltpu.VMEM((features, tokens), bf16),
            pltpu.VMEM((TILE + tokens, LANES), f32),
            pltpu.VMEM((4, tokens // LANES, 8, LANES), f32),
            pltpu.VMEM((nz, 8, LANES), f32),
            pltpu.VMEM((nz, 8, LANES), f32),
            pltpu.VMEM((tiles, 8, LANES), f32),
            pltpu.VMEM((nw, 8, LANES), f32),
            pltpu.VMEM((nz, 1, LANES), f32),
            pltpu.VMEM((tiles, nz, 1, LANES), f32),
            [pltpu.VMEM((features, n), f32) for n in WIDTHS],
            [pltpu.VMEM((2, part // 2, n), f32) for n in WIDTHS],
            [pltpu.VMEM((2, part, n), f32) for n in WIDTHS],
            [pltpu.VMEM((part, n), f32) for n in WIDTHS],
            pltpu.VMEM((ny - 1, part, WIDTHS[-1]), f32),
            dma((chunks + 2,)), dma((chunks,)),
            dma((2 * nx,)), dma((2 * nx,)),
            dma((2, chunks)),
            dma((2, chunks, steps)), dma((2, chunks, steps)),
            dma((nz,)), dma((nz,)),
            dma((tiles,)), dma((nw,)),
            dma((nw,)), dma((tiles,)),
            dma((nz,)), dma((nz,)),
            *[dma((chunks, 2))] * 8,
            dma((4, ny - 1)),
        ],
        compiler_params=pltpu.CompilerParams(
            collective_id=0, has_side_effects=True, vmem_limit_bytes=50 * 1024 * 1024
        ),
        cost_estimate=pl.CostEstimate(
            flops=2 * tokens * features * hidden, bytes_accessed=1 << 23, transcendentals=0
        ),
    )(*stay, clip_bound)


def solution(mesh):
    sizes = tuple(mesh.shape[a] for a in ("dp", "row", "col"))

    def run(activations, out_grads, query_ids, clip_bound):
        placed = (P("dp", "col", "row"), P("dp", "row", "col"), P("dp", None), P())
        return jax.shard_map(
            functools.partial(body, sizes + (query_ids.shape[1],)),
            mesh=mesh, in_specs=placed, out_specs=P("row", "col"), check_vma=False,
        )(activations, out_grads, query_ids, clip_bound)

    return run
```

profile of v0, /device:TPU:8, one launch (start us, length us, event | category | flops | bytes accessed | tf_op | source)
XLA Modules:
  0.0 155.8 jit_solution(14979807282709833929)
XLA Ops:
  0.7 153.9 %shard_map.46 = f32[256,1792]{1,0:T(8,128)S(1)} custom-call(bf16[384,256]{1,0:T(8,128)(2,1)} %bitcast.3, bf16[192,1792]{1,0:T(8,128)(2,1)} %bitcast.2, s32[1,3072]{1,0:T(1,128)} %ids_ref.1, s32[1]{0:T(128)S(6)} %copy.6.clip_ref), custom_call_target="tpu_custom_call" | custom-call | flops 2818572288 | bytes 8388608 | tf_op jit(solution)/shard_map/pallas_call | solution.py:541
  154.6 1.2 copy.7
where the time goes:
time: 156 us
  Pallas kernels  154 us (99%)
    pallas_call x1, Pallas kernels, body(): pl.pallas_call(functools.partial(kernel, sizes), out_shape=jax.ShapeDtype...  154 us

commit v1 on v0

--- a/solution.py
+++ b/solution.py
@@ -9,9 +9,10 @@
 
 TILE = 32
 LANES = 128
-WIDTHS = (256, 256, 256, 128, 256, 256, 256, 128)
-FIRST_SLOTS = (0, 0, 0, 1, 4, 5, 7, 8)
-STAGE_GAP = 3
+WIDTHS = (256, 256, 256, 256, 256, 256, 256)
+FIRST_SLOTS = (0, 0, 0, 1, 3, 6, 7)
+STAGE_GAP = 2
+DIRECT = 2
 MESH = pl.DeviceIdType.MESH
 
 
@@ -42,6 +43,7 @@
     tc = x_ref.shape[0]
     tiles = tz // TILE
     chunks = len(WIDTHS)
+    plain = chunks - DIRECT
     columns = [pl.ds(sum(WIDTHS[:c]), WIDTHS[c]) for c in range(chunks)]
     steps = nz // 2
     wide = bands.shape[1]
@@ -199,13 +201,15 @@
     def direct_send(c, d):
         to = y_at(d)
         return copy_to(
-            pbuf[c].at[quarter(to)], rdir.at[d - 1], sd.at[0, d - 1], sd.at[1, d - 1], dp=to
+            pbuf[c].at[quarter(to)], rdir[c - plain].at[d - 1],
+            sd.at[0, c - plain, d - 1], sd.at[1, c - plain, d - 1], dp=to,
         )
 
     def direct_out(c, d, incoming=False):
         at = out_at(c, quarter(y_at(ny - d) if incoming else y))
         return copy_to(
-            at if incoming else qbuf[c], at, sd.at[2, d - 1], sd.at[3, d - 1], dp=y_at(d)
+            at if incoming else qbuf[c], at,
+            sd.at[2, c - plain, d - 1], sd.at[3, c - plain, d - 1], dp=y_at(d),
         )
 
     def out_own(c):
@@ -243,7 +247,7 @@
         total = pbuf[c][quarter(y)]
         for d in range(1, ny):
             direct_send(c, d).wait_recv()
-            total = total + rdir[d - 1]
+            total = total + rdir[c - plain][d - 1]
         qbuf[c][...] = total
         for d in range(1, ny):
             direct_out(c, d).start()
@@ -462,7 +466,7 @@
     def first(c):
         for way in range(2):
             ring(way, c, steps - 1, incoming=True).wait_recv()
-        if c == chunks - 1:
+        if c >= plain:
             product_rest(c)
         else:
             product(c)
@@ -471,7 +475,7 @@
     def stages(p):
         for c in range(chunks):
             calls = (first, near, finish, forward_out, out_done)
-            if c == chunks - 1:
+            if c >= plain:
                 calls = (first, direct_finish, direct_done)
             stage, rest = divmod(p - 2 * (first_slot[c] + steps) - c % 2, STAGE_GAP)
             if 0 <= stage < len(calls) and rest == 0:
@@ -496,7 +500,9 @@
         for c in range(1, chunks, 2):
             hop(t, c)
         stages(2 * t + 1)
-    product_most(chunks - 1)
+        for c in range(plain, chunks):
+            if t == first_slot[c] + steps - 1:
+                product_most(c)
 
     for c in range(chunks):
         halo_copy(c).wait_send()
@@ -566,7 +572,7 @@
             [pltpu.VMEM((2, part // 2, n), f32) for n in WIDTHS],
             [pltpu.VMEM((2, part, n), f32) for n in WIDTHS],
             [pltpu.VMEM((part, n), f32) for n in WIDTHS],
-            pltpu.VMEM((ny - 1, part, WIDTHS[-1]), f32),
+            [pltpu.VMEM((ny - 1, part, n), f32) for n in WIDTHS[-DIRECT:]],
             dma((chunks + 2,)), dma((chunks,)),
             dma((2 * nx,)), dma((2 * nx,)),
             dma((2, chunks)),
@@ -576,7 +582,7 @@
             dma((nw,)), dma((tiles,)),
             dma((nz,)), dma((nz,)),
             *[dma((chunks, 2))] * 8,
-            dma((4, ny - 1)),
+            dma((4, DIRECT, ny - 1)),
         ],
         compiler_params=pltpu.CompilerParams(
             collective_id=0, has_side_effects=True, vmem_limit_bytes=50 * 1024 * 1024

time: 156 us -> 153 us (0.981)
  the two profiles are of different devices: /device:TPU:8 before, /device:TPU:4 now
where the time goes in v1:
time: 153 us
  Pallas kernels  151 us (99%)
    pallas_call x1, Pallas kernels, body(): pl.pallas_call(functools.partial(kernel, sizes), out_shape=jax.ShapeDtype...  151 us

profile of v1, /device:TPU:4, one launch (start us, length us, event | category | flops | bytes accessed | tf_op | source)
XLA Modules:
  0.0 152.7 jit_solution(5515710758286197716)
XLA Ops:
  0.7 150.8 %shard_map.46 = f32[256,1792]{1,0:T(8,128)S(1)} custom-call(bf16[384,256]{1,0:T(8,128)(2,1)} %bitcast.3, bf16[192,1792]{1,0:T(8,128)(2,1)} %bitcast.2, s32[1,3072]{1,0:T(1,128)} %ids_ref.1, s32[1]{0:T(128)S(6)} %copy.6.clip_ref), custom_call_target="tpu_custom_call" | custom-call | flops 2818572288 | bytes 8388608 | tf_op jit(solution)/shard_map/pallas_call | solution.py:547
  151.4 1.2 copy.7

commit v2 on v1

--- a/solution.py
+++ b/solution.py
@@ -13,6 +13,8 @@
 FIRST_SLOTS = (0, 0, 0, 1, 3, 6, 7)
 STAGE_GAP = 2
 DIRECT = 2
+SPLIT = 3
+AHEAD = 3
 MESH = pl.DeviceIdType.MESH
 
 
@@ -240,8 +242,12 @@
 
     def product_rest(c):
         pbuf[c][...] = pbuf[c][...] + product_pair(c, 0)
-        for d in range(1, ny):
-            direct_send(c, d).start()
+        if c < plain:
+            for side in range(2):
+                far_send(c, side).start()
+        else:
+            for d in range(1, ny):
+                direct_send(c, d).start()
 
     def direct_finish(c):
         total = pbuf[c][quarter(y)]
@@ -461,12 +467,17 @@
             for way in range(2):
                 if s > 0:
                     ring(way, c, s - 1, incoming=True).wait_recv()
-                ring(way, c, s).start()
+                if (s, c) == (0, AHEAD):
+                    @pl.when(core == 1)
+                    def _():
+                        ring(way, c, s).start()
+                else:
+                    ring(way, c, s).start()
 
     def first(c):
         for way in range(2):
             ring(way, c, steps - 1, incoming=True).wait_recv()
-        if c >= plain:
+        if c >= chunks - SPLIT:
             product_rest(c)
         else:
             product(c)
@@ -489,6 +500,10 @@
         for c in range(0, chunks, 2):
             hop(t, c)
         if t == 0:
+            @pl.when(core == 0)
+            def _():
+                for way in range(2):
+                    ring(way, AHEAD, 0).start()
             for d in range(nx):
                 x_first(d).start()
             for c in range(chunks):
@@ -500,7 +515,7 @@
         for c in range(1, chunks, 2):
             hop(t, c)
         stages(2 * t + 1)
-        for c in range(plain, chunks):
+        for c in range(chunks - SPLIT, chunks):
             if t == first_slot[c] + steps - 1:
                 product_most(c)
 

time: 153 us -> 153 us (level)
  the two profiles are of different devices: /device:TPU:4 before, /device:TPU:2 now
where the time goes in v2:
time: 153 us
  Pallas kernels  151 us (99%)
    pallas_call x1, Pallas kernels, body(): pl.pallas_call(functools.partial(kernel, sizes), out_shape=jax.ShapeDtype...  151 us

profile of v2, /device:TPU:2, one launch (start us, length us, event | category | flops | bytes accessed | tf_op | source)
XLA Modules:
  0.0 152.8 jit_solution(10239731910508493986)
XLA Ops:
  0.7 150.9 %shard_map.46 = f32[256,1792]{1,0:T(8,128)S(1)} custom-call(bf16[384,256]{1,0:T(8,128)(2,1)} %bitcast.3, bf16[192,1792]{1,0:T(8,128)(2,1)} %bitcast.2, s32[1,3072]{1,0:T(1,128)} %ids_ref.1, s32[1]{0:T(128)S(6)} %copy.6.clip_ref), custom_call_target="tpu_custom_call" | custom-call | flops 2818572288 | bytes 8388608 | tf_op jit(solution)/shard_map/pallas_call | solution.py:562
  151.6 1.2 copy.7

commit v3 on v1

--- a/solution.py
+++ b/solution.py
@@ -10,7 +10,7 @@
 TILE = 32
 LANES = 128
 WIDTHS = (256, 256, 256, 256, 256, 256, 256)
-FIRST_SLOTS = (0, 0, 0, 1, 3, 6, 7)
+FIRST_SLOTS = (0, 0, 0, 1, 2, 6, 7)
 STAGE_GAP = 2
 DIRECT = 2
 MESH = pl.DeviceIdType.MESH

time: 153 us -> 153 us (level)
  the two profiles are of different devices: /device:TPU:4 before, /device:TPU:2 now
where the time goes in v3:
time: 153 us
  Pallas kernels  151 us (99%)
    pallas_call x1, Pallas kernels, body(): pl.pallas_call(functools.partial(kernel, sizes), out_shape=jax.ShapeDtype...  151 us

profile of v3, /device:TPU:2, one launch (start us, length us, event | category | flops | bytes accessed | tf_op | source)
XLA Modules:
  0.0 153.3 jit_solution(11730986374651009216)
XLA Ops:
  0.7 151.4 %shard_map.46 = f32[256,1792]{1,0:T(8,128)S(1)} custom-call(bf16[384,256]{1,0:T(8,128)(2,1)} %bitcast.3, bf16[192,1792]{1,0:T(8,128)(2,1)} %bitcast.2, s32[1,3072]{1,0:T(1,128)} %ids_ref.1, s32[1]{0:T(128)S(6)} %copy.6.clip_ref), custom_call_target="tpu_custom_call" | custom-call | flops 2818572288 | bytes 8388608 | tf_op jit(solution)/shard_map/pallas_call | solution.py:547
  152.1 1.2 copy.7

commit v4 on v2

--- a/solution.py
+++ b/solution.py
@@ -14,7 +14,6 @@
 STAGE_GAP = 2
 DIRECT = 2
 SPLIT = 3
-AHEAD = 3
 MESH = pl.DeviceIdType.MESH
 
 
@@ -467,12 +466,7 @@
             for way in range(2):
                 if s > 0:
                     ring(way, c, s - 1, incoming=True).wait_recv()
-                if (s, c) == (0, AHEAD):
-                    @pl.when(core == 1)
-                    def _():
-                        ring(way, c, s).start()
-                else:
-                    ring(way, c, s).start()
+                ring(way, c, s).start()
 
     def first(c):
         for way in range(2):
@@ -500,10 +494,6 @@
         for c in range(0, chunks, 2):
             hop(t, c)
         if t == 0:
-            @pl.when(core == 0)
-            def _():
-                for way in range(2):
-                    ring(way, AHEAD, 0).start()
             for d in range(nx):
                 x_first(d).start()
             for c in range(chunks):

time: 153 us -> 153 us (level)
  no operation moved by 1% of the time
where the time goes in v4:
time: 153 us
  Pallas kernels  151 us (99%)
    pallas_call x1, Pallas kernels, body(): pl.pallas_call(functools.partial(kernel, sizes), out_shape=jax.ShapeDtype...  151 us

profile of v4, /device:TPU:2, one launch (start us, length us, event | category | flops | bytes accessed | tf_op | source)
XLA Modules:
  0.0 152.7 jit_solution(13153031556770835)
XLA Ops:
  0.7 150.8 %shard_map.46 = f32[256,1792]{1,0:T(8,128)S(1)} custom-call(bf16[384,256]{1,0:T(8,128)(2,1)} %bitcast.3, bf16[192,1792]{1,0:T(8,128)(2,1)} %bitcast.2, s32[1,3072]{1,0:T(1,128)} %ids_ref.1, s32[1]{0:T(128)S(6)} %copy.6.clip_ref), custom_call_target="tpu_custom_call" | custom-call | flops 2818572288 | bytes 8388608 | tf_op jit(solution)/shard_map/pallas_call | solution.py:552
  151.4 1.2 copy.7
